TPU v7x, 32 devices: a whole 2x2x4 slice. The times are simulated.
32 devices in a mesh: seq: 8 (over y, x, core), hid: 4 (over z).
Axes of the slice: x: 2, y: 2, z: 4, core: 2. Of those that a mesh axis runs over, the one named last changes fastest.
Arguments:
- skip_stream: bfloat16 [1024, 4096], P('seq', 'hid'), may hold values from -6 to 6
- acceptance_signal: bfloat16 [1024, 4096], P('seq', 'hid'), may hold values from -6 to 6
- attention_lookups: bfloat16 [1024, 4096], P('seq', 'hid'), may hold values from -6 to 6
- attention_payloads: bfloat16 [1024, 4096], P('seq', 'hid'), may hold values from -6 to 6
- output_gating: bfloat16 [1024, 4096], P('seq', 'hid'), may hold values from -6 to 6
- forgetting_logit: float32 [1024, 4096], P('seq', 'hid'), may hold values from -16 to 0
- present_boost: float32 [64, 64], P('hid'), may hold values from -4 to 4
- groupwise_scaling: float32 [4096], P('hid'), may hold values from 0.1 to 1.9
- groupwise_offset: float32 [4096], P('hid'), may hold values from -3 to 3
- normalizer_scaling: float32 [4096], P('hid'), may hold values from 0.1 to 1.9
- normalizer_offset: float32 [4096], P('hid'), may hold values from -3 to 3
- lagged_blend_factor: float32 [4096], P('hid'), may hold values from 0.1 to 0.9
- feedforward_query_matrix: bfloat16 [4096, 7168], P('seq', 'hid'), may hold values from -0.09375 to 0.09375
- feedforward_output_matrix: bfloat16 [4096, 7168], P('seq', 'hid'), may hold values from -0.09375 to 0.09375
Outputs:
- block_out: bfloat16 [1024, 4096], P('seq', 'hid')
All inputs are finite; a program needn't handle non-finite values.
Results may differ from a plain program's by a relative error of at most 0.019.
Values may be sent and summed in bfloat16 or wider, within the bound.
A program may use at most 128 MiB of HBM per device.

v0:
```python
import jax
import jax.numpy as jnp
from jax import lax
from jax.sharding import PartitionSpec as P

EPS_GROUP = 0.00064
EPS_LAYER = 1e-05
HIGH_PRECISION = lax.Precision.HIGHEST


def shifted(block, axis, distance):
    devices = range(lax.axis_size(axis))
    route = [(i - distance, i) for i in devices if i - distance in devices]
    return lax.ppermute(block, axis, route)


def lookup_payload_outer(
    memory_matrix, acceptance_product, key, payload_entries, forgetting_exponent, present_boost
):
    span = acceptance_product.shape[0]
    inclusive_prefix = jnp.cumsum(forgetting_exponent, axis=0)
    exclusive_prefix = inclusive_prefix - forgetting_exponent
    differ = exclusive_prefix[:, None] - inclusive_prefix[None, :]
    later = jnp.arange(span)[:, None] > jnp.arange(span)[None, :]
    factor = jnp.where(later[:, :, None, None], jnp.exp(jnp.minimum(differ, 0.0)), 0.0)
    scores = jnp.einsum(
        "thk,tshk,shk->tsh", acceptance_product, factor, key, precision=HIGH_PRECISION
    )
    inside_segment = jnp.sum(acceptance_product * present_boost[None] * key, axis=-1)
    block_result = (
        jnp.einsum("tsh,shv->thv", scores, payload_entries, precision=HIGH_PRECISION)
        + inside_segment[..., None] * payload_entries
    )
    block_result = block_result + jnp.einsum(
        "jsn,snm->jsm",
        acceptance_product * jnp.exp(exclusive_prefix),
        memory_matrix,
        precision=HIGH_PRECISION,
    )
    trailing_rows = jnp.exp(inclusive_prefix[-1][None] - inclusive_prefix)
    memory_matrix = jnp.exp(inclusive_prefix[-1])[..., None] * memory_matrix + jnp.einsum(
        "gte,gtc->tec", key * trailing_rows, payload_entries, precision=HIGH_PRECISION
    )
    return (memory_matrix, block_result)


def local(
    skip_stream,
    acceptance_signal,
    attention_lookups,
    attention_payloads,
    output_gating,
    forgetting_logit,
    present_boost,
    groupwise_scaling,
    groupwise_offset,
    normalizer_scaling,
    normalizer_offset,
    lagged_blend_factor,
    feedforward_query_matrix,
    feedforward_output_matrix,
):
    rows, width = skip_stream.shape
    subspace_slices, subspace_ordinal = present_boost.shape
    span = min(64, rows)
    count = rows // span

    def split(a):
        return a.astype(jnp.float32).reshape(count, span, subspace_slices, subspace_ordinal)

    forgetting_exponent = -jnp.exp(forgetting_logit)
    blocks = (
        split(acceptance_signal),
        split(attention_lookups),
        split(attention_payloads),
        forgetting_exponent.reshape(count, span, subspace_slices, subspace_ordinal),
    )

    def step(memory_matrix, segment_ordinal):
        return lookup_payload_outer(
            memory_matrix,
            segment_ordinal[0],
            segment_ordinal[1],
            segment_ordinal[2],
            segment_ordinal[3],
            present_boost,
        )

    zero_state = jnp.zeros((subspace_slices, subspace_ordinal, subspace_ordinal), jnp.float32)
    local_state, pieces = lax.scan(step, zero_state, blocks)
    wkv = pieces.reshape(rows, subspace_slices, subspace_ordinal)
    logw_rows = forgetting_exponent.reshape(rows, subspace_slices, subspace_ordinal)
    total = jnp.sum(logw_rows, axis=0)
    preceding_rows = jnp.cumsum(logw_rows, axis=0) - logw_rows
    every_state, totals_all = (
        lax.all_gather(local_state[None].astype(jnp.bfloat16), "seq", axis=0, tiled=True).astype(
            jnp.float32
        ),
        lax.all_gather(total[None].astype(jnp.bfloat16), "seq", axis=0, tiled=True).astype(
            jnp.float32
        ),
    )
    mine = lax.axis_index("seq")
    ends = jnp.cumsum(totals_all, axis=0)
    starts = ends - totals_all
    here = lax.dynamic_index_in_dim(starts, mine, 0, keepdims=False)
    earlier = jnp.arange(totals_all.shape[0]) < mine
    decay_weights = jnp.where(
        earlier[:, None, None], jnp.exp(jnp.minimum(here[None] - ends, 0.0)), 0.0
    )
    incoming_state = jnp.einsum(
        "scw,scwp->cwp", decay_weights, every_state, precision=HIGH_PRECISION
    )
    receptance_rows = acceptance_signal.astype(jnp.float32).reshape(
        rows, subspace_slices, subspace_ordinal
    )
    wkv = wkv + jnp.einsum(
        "jsn,snm->jsm",
        receptance_rows * jnp.exp(preceding_rows),
        incoming_state,
        precision=HIGH_PRECISION,
    )
    centre = wkv - jnp.mean(wkv, axis=-1, keepdims=True)
    spread = jnp.mean(centre * centre, axis=-1, keepdims=True)
    normed = (centre * lax.rsqrt(spread + EPS_GROUP)).reshape(rows, width)
    normed = normed * groupwise_scaling + groupwise_offset
    middle = skip_stream.astype(jnp.float32) + normed * jax.nn.silu(
        output_gating.astype(jnp.float32)
    )
    first, second = lax.psum(
        (jnp.sum(middle, axis=1, keepdims=True), jnp.sum(middle * middle, axis=1, keepdims=True)),
        "hid",
    )
    full_width = width * lax.axis_size("hid")
    mean_row = first / full_width
    var_row = second / full_width - mean_row * mean_row
    xn = (
        (middle - mean_row) * lax.rsqrt(var_row + EPS_LAYER) * normalizer_scaling
        + normalizer_offset
    ).astype(jnp.bfloat16)
    carried_row = shifted(xn[rows - 1 :], "seq", 1)
    prev = jnp.concatenate([carried_row, xn[: rows - 1]], axis=0)
    xn_wide = xn.astype(jnp.float32)
    xk = (xn_wide + (prev.astype(jnp.float32) - xn_wide) * lagged_blend_factor).astype(jnp.bfloat16)
    whole = lax.all_gather(xk, "hid", axis=1, tiled=True)
    pre = jnp.dot(
        whole,
        lax.all_gather(feedforward_query_matrix, "seq", axis=0, tiled=True),
        preferred_element_type=jnp.float32,
    )
    hidden = jnp.square(jnp.maximum(pre, 0.0)).astype(jnp.bfloat16)
    down = lax.dot_general(
        hidden,
        lax.all_gather(feedforward_output_matrix, "seq", axis=0, tiled=True),
        (((1,), (1,)), ((), ())),
        preferred_element_type=jnp.float32,
    )
    mixed = lax.psum_scatter(
        down.astype(jnp.bfloat16), "hid", scatter_dimension=1, tiled=True
    ).astype(jnp.float32)
    return (middle + mixed).astype(jnp.bfloat16)


def solution(mesh):
    return jax.shard_map(
        local,
        mesh=mesh,
        in_specs=(
            P("seq", "hid"),
            P("seq", "hid"),
            P("seq", "hid"),
            P("seq", "hid"),
            P("seq", "hid"),
            P("seq", "hid"),
            P("hid", None),
            P("hid"),
            P("hid"),
            P("hid"),
            P("hid"),
            P("hid"),
            P("seq", "hid"),
            P("seq", "hid"),
        ),
        out_specs=P("seq", "hid"),
        check_vma=False,
    )
```

profile of v0, /device:TPU:24, one launch (start us, length us, event | category | flops | bytes accessed | tf_op | source)
XLA Modules:
  0.0 539.6 jit_solution(6563220086733012146)
XLA Ops:
  9.6 2.2 reshape.108
  11.8 2.2 reshape.110
  16.8 216.7 %while.13 = (s32[]{:T(128)}, f32[16,64,64]{2,1,0:T(8,128)S(1)}, f32[2,64,16,64]{1,0,3,2:T(2,128)}, f32[2,64,16,64]{1,0,3,2:T(2,128)}, f32[2,64,16,64]{3,2,1,0:T(...) while((s32[]{:T(128)}, f32[16,64,64]{2,1,0:T(8,128)S(1)}, ...), condition=%wide.region_3.4_spmd.clone, body=%wide.region_0.3_spmd.clone.sunk | while | flops 223153152 | bytes 47763648 | solution.py:90
  16.8 2.6 constant_dynamic-slice_fusion.5
  21.5 6.3 %fusion.63 = f32[64,16,64]{2,1,0:T(8,128)S(1)} fusion(f32[1,64,16,64]{3,2,1,0:T(8,128)S(1)} %copy.119), kind=kOutput, calls=%fused_computation.16.clone.1 | output fusion | flops 4128768 | bytes 524288 | tf_op jit(solution)/shard_map/while/body/eval_jaxpr/jit(cumsum)/reduce_window_sum | solution.py:21
  28.8 11.4 %multiply_bitcast_fusion.3 = f32[64,16,64,64]{2,1,0,3:T(8,128)} fusion(f32[64,16,64]{2,1,0:T(8,128)S(1)} %get-tuple-element.185, f32[64,16,64]{2,1,0:T(8,128)S(1)} %fusion.63, f32[64,16,64]{2,1,0:T(8,128)S(1)} %get-tuple-element.187, pred[64,64]{1,0:T(8,128)(4,1)S(1)} %iota_compare_fusion.3), kind=kLoop, calls=%fused_computation.2.clone.1 | loop fusion | flops 16777216 | bytes 17567744 | tf_op jit(solution)/shard_map/while/body/eval_jaxpr/thk,tshk,shk->tsh/dot_general | solution.py:26
  40.2 66.1 %fusion.66 = f32[64,16,1,64]{3,2,1,0:T(1,128)S(1)} fusion(f32[64,16,64,1]{2,3,1,0:T(1,128)S(1)} %bitcast.111, f32[64,16,64,64]{2,1,0,3:T(8,128)} %multiply_bitcast_fusion.3), kind=kOutput, calls=%fused_computation.clone.1 | convolution fusion | flops 50331648 | bytes 17301504 | tf_op jit(solution)/shard_map/while/body/eval_jaxpr/thk,tshk,shk->tsh/dot_general | solution.py:26
  111.8 13.4 %dynamic_update_slice.6 = f32[2,64,16,64]{1,0,3,2:T(2,128)} dynamic-update-slice(f32[2,64,16,64]{1,0,3,2:T(2,128)} %get-tuple-element.202, f32[1,64,16,64]{1,0,3,2:T(1,128)S(1)} %copy.121, s32[]{:T(128)S(6)} %copy.126, s32[]{:T(128)} %constant.48.clone.1..sunk, s32[]{:T(128)} %constant.48.clone.1..sunk, s32[]{:T(128)} %constant.48.clone.1..sunk) | dynamic-update-slice | bytes 524292 | tf_op jit(solution)/shard_map/while/body/jit(dynamic_update_index_in_dim)/dynamic_update_slice | solution.py:90
  125.1 2.6 constant_dynamic-slice_fusion.5
  129.9 6.3 %fusion.63 = f32[64,16,64]{2,1,0:T(8,128)S(1)} fusion(f32[1,64,16,64]{3,2,1,0:T(8,128)S(1)} %copy.119), kind=kOutput, calls=%fused_computation.16.clone.1 | output fusion | flops 4128768 | bytes 524288 | tf_op jit(solution)/shard_map/while/body/eval_jaxpr/jit(cumsum)/reduce_window_sum | solution.py:21
  137.2 11.4 %multiply_bitcast_fusion.3 = f32[64,16,64,64]{2,1,0,3:T(8,128)} fusion(f32[64,16,64]{2,1,0:T(8,128)S(1)} %get-tuple-element.185, f32[64,16,64]{2,1,0:T(8,128)S(1)} %fusion.63, f32[64,16,64]{2,1,0:T(8,128)S(1)} %get-tuple-element.187, pred[64,64]{1,0:T(8,128)(4,1)S(1)} %iota_compare_fusion.3), kind=kLoop, calls=%fused_computation.2.clone.1 | loop fusion | flops 16777216 | bytes 17567744 | tf_op jit(solution)/shard_map/while/body/eval_jaxpr/thk,tshk,shk->tsh/dot_general | solution.py:26
  148.5 66.1 %fusion.66 = f32[64,16,1,64]{3,2,1,0:T(1,128)S(1)} fusion(f32[64,16,64,1]{2,3,1,0:T(1,128)S(1)} %bitcast.111, f32[64,16,64,64]{2,1,0,3:T(8,128)} %multiply_bitcast_fusion.3), kind=kOutput, calls=%fused_computation.clone.1 | convolution fusion | flops 50331648 | bytes 17301504 | tf_op jit(solution)/shard_map/while/body/eval_jaxpr/thk,tshk,shk->tsh/dot_general | solution.py:26
  220.1 13.4 %dynamic_update_slice.6 = f32[2,64,16,64]{1,0,3,2:T(2,128)} dynamic-update-slice(f32[2,64,16,64]{1,0,3,2:T(2,128)} %get-tuple-element.202, f32[1,64,16,64]{1,0,3,2:T(1,128)S(1)} %copy.121, s32[]{:T(128)S(6)} %copy.126, s32[]{:T(128)} %constant.48.clone.1..sunk, s32[]{:T(128)} %constant.48.clone.1..sunk, s32[]{:T(128)} %constant.48.clone.1..sunk) | dynamic-update-slice | bytes 524292 | tf_op jit(solution)/shard_map/while/body/jit(dynamic_update_index_in_dim)/dynamic_update_slice | solution.py:90
  234.4 2.7 reshape.103
  237.1 9.1 %all_gather.15 = bf16[8,16,64]{2,1,0:T(8,128)(2,1)S(1)} all-gather(bf16[1,16,64]{2,1,0:T(8,128)(2,1)S(1)} %convert_element_type.63), channel_id=1, replica_groups=mesh['seq'=8,'hid'=4] {'seq'}, dimensions={0}, use_global_device_ids=true | all-gather | bytes 18432 | tf_op jit(solution)/shard_map/all_gather | solution.py:99
  248.4 23.9 %exponential_multiply_fusion.1 = f32[128,16,64]{2,1,0:T(8,128)S(1)} fusion(f32[128,16,64]{2,1,0:T(8,128)S(1)} %copy.50, f32[128,16,64]{2,1,0:T(8,128)S(1)} %copy.48), kind=kOutput, calls=%fused_computation.41 | output fusion | flops 16908288 | bytes 1572864 | tf_op jit(solution)/shard_map/jit(cumsum)/reduce_window_sum | solution.py:94
  272.3 2.5 multiply_reduce_fusion
  274.9 3.4 fusion.36
  279.9 8.1 %all-reduce = (f32[128,1]{0,1:T(1,128)S(1)}, f32[128,1]{0,1:T(1,128)S(1)}) all-reduce(f32[128,1]{0,1:T(1,128)S(1)} %bitcast.118, f32[128,1]{0,1:T(1,128)S(1)} %bitcast.117), channel_id=1, replica_groups=mesh['seq'=8,'hid'=4] {'hid'}, use_global_device_ids=true, to_apply=%region_12.13 | all-reduce | flops 256 | bytes 2048 | tf_op jit(solution)/shard_map/psum | solution.py:130
  292.7 29.9 %all-gather.6.cloned.1.call-done = bf16[128,4096]{1,0:T(8,128)(2,1)} async-done(((bf16[128,1024]{1,0:T(8,128)(2,1)}), bf16[128,4096]{1,0:T(8,128)(2,1)}) %all-gather.6.cloned.1.call-update) | async-done | bytes 1048592 | tf_op jit(solution)/shard_map/all_gather | solution.py:145
  322.5 83.8 %all-gather.10.cloned.1.call-done = bf16[4096,1792]{1,0:T(8,128)(2,1)} async-done(((bf16[512,1792]{1,0:T(8,128)(2,1)}), bf16[4096,1792]{1,0:T(8,128)(2,1)}) %all-gather.10.cloned.1.call-update) | async-done | bytes 14680080 | tf_op jit(solution)/shard_map/all_gather | solution.py:154
  406.4 82.8 %all-gather.8.cloned.1.call-done = bf16[4096,1792]{1,0:T(8,128)(2,1)} async-done(((bf16[512,1792]{1,0:T(8,128)(2,1)}), bf16[4096,1792]{1,0:T(8,128)(2,1)}) %all-gather.8.cloned.1.call-update) | async-done | bytes 14680080 | tf_op jit(solution)/shard_map/all_gather | solution.py:148
  489.1 17.2 %convolution_convert_fusion = bf16[128,4096]{1,0:T(8,128)(2,1)} fusion(bf16[4096,1792]{1,0:T(8,128)(2,1)} %all-gather.10.cloned.1.call-done, bf16[128,4096]{1,0:T(8,128)(2,1)} %all-gather.6.cloned.1.call-done, bf16[4096,1792]{1,0:T(8,128)(2,1)} %all-gather.8.cloned.1.call-done), kind=kOutput, calls=%fused_computation.33 | convolution fusion | flops 3759308800 | bytes 31457280 | tf_op jit(solution)/shard_map/dot_general | solution.py:152
  506.3 25.0 %reduce-scatter.2.cloned.1.call-done = bf16[128,1024]{1,0:T(8,128)(2,1)} async-done(((bf16[128,4096]{1,0:T(8,128)(2,1)}), bf16[128,1024]{1,0:T(8,128)(2,1)}) %reduce-scatter.2.cloned.1.call-update) | async-done | bytes 262160 | tf_op jit(solution)/shard_map/reduce_scatter | solution.py:158
  (90 shorter events, 33.8 us)
Async XLA Ops:
  6.5 265.8 %all-gather.12.cloned.1.call-start = ((), (), s32[]{:S(2)}) async-start(), calls=%async_computation.5 | async-start | bytes 2359296 | tf_op jit(solution)/shard_map/all_gather | solution.py:96
  8.0 8.8 %copy-start.2 = (f32[128,1024]{0,1:T(8,128)}, f32[128,1024]{0,1:T(8,128)S(1)}, u32[]{:S(2)}) copy-start(f32[128,1024]{0,1:T(8,128)S(1)} %get-tuple-element.122) | copy-start | bytes 1572868
  40.2 66.1 %copy-start.1 = (f32[2,64,16,64]{3,2,1,0:T(8,128)S(1)}, f32[2,64,16,64]{3,2,1,0:T(8,128)}, u32[]{:S(2)}) copy-start(f32[2,64,16,64]{3,2,1,0:T(8,128)} %get-tuple-element.215) | copy-start | bytes 1572868 | tf_op jit(solution)/shard_map/while
  40.2 68.1 %copy-start = (f32[64,16,64]{2,1,0:T(8,128)S(1)}, f32[64,16,64]{2,1,0:T(8,128)}, u32[]{:S(2)}) copy-start(f32[64,16,64]{2,1,0:T(8,128)} %get-tuple-element.189) | copy-start | bytes 786436 | tf_op jit(solution)/shard_map/while
  148.5 66.1 %copy-start.1 = (f32[2,64,16,64]{3,2,1,0:T(8,128)S(1)}, f32[2,64,16,64]{3,2,1,0:T(8,128)}, u32[]{:S(2)}) copy-start(f32[2,64,16,64]{3,2,1,0:T(8,128)} %get-tuple-element.215) | copy-start | bytes 1572868 | tf_op jit(solution)/shard_map/while
  148.5 68.1 %copy-start = (f32[64,16,64]{2,1,0:T(8,128)S(1)}, f32[64,16,64]{2,1,0:T(8,128)}, u32[]{:S(2)}) copy-start(f32[64,16,64]{2,1,0:T(8,128)} %get-tuple-element.189) | copy-start | bytes 786436 | tf_op jit(solution)/shard_map/while
  233.5 45.1 %copy-start.6 = (f32[1024]{0:T(1024)S(1)}, f32[1024]{0:T(1024)}, u32[]{:S(2)}) copy-start(f32[1024]{0:T(1024)} %param.24) | copy-start | bytes 12292
  233.5 45.1 %copy-start.7 = (f32[1024]{0:T(1024)S(1)}, f32[1024]{0:T(1024)}, u32[]{:S(2)}) copy-start(f32[1024]{0:T(1024)} %param.23) | copy-start | bytes 12292
  233.5 54.6 %copy-start.4 = (f32[1024]{0:T(1024)S(1)}, f32[1024]{0:T(1024)}, u32[]{:S(2)}) copy-start(f32[1024]{0:T(1024)} %param.26) | copy-start | bytes 12292
  233.5 54.6 %copy-start.5 = (f32[1024]{0:T(1024)S(1)}, f32[1024]{0:T(1024)}, u32[]{:S(2)}) copy-start(f32[1024]{0:T(1024)} %param.25) | copy-start | bytes 12292
  233.5 56.8 %copy-start.8 = (f32[1024]{0:T(1024)S(1)}, f32[1024]{0:T(1024)}, u32[]{:S(2)}) copy-start(f32[1024]{0:T(1024)} %param.27) | copy-start | bytes 12292
  234.3 88.3 %all-gather.6.cloned.1.call-start = ((), (), s32[]{:S(2)}) async-start(), calls=%async_computation.1 | async-start | bytes 1310720 | tf_op jit(solution)/shard_map/all_gather | solution.py:145
  234.4 44.3 %copy-start.3 = (bf16[128,1024]{1,0:T(8,128)(2,1)S(1)}, bf16[128,1024]{1,0:T(8,128)(2,1)}, u32[]{:S(2)}) copy-start(bf16[128,1024]{1,0:T(8,128)(2,1)} %param.20) | copy-start | bytes 786436
  288.2 2.1 collective-permute-start
  291.3 115.1 %all-gather.10.cloned.1.call-start = ((), (), s32[]{:S(2)}) async-start(), calls=%async_computation.3 | async-start | bytes 16515072 | tf_op jit(solution)/shard_map/all_gather | solution.py:154
  292.1 197.1 %all-gather.8.cloned.1.call-start = ((), (), s32[]{:S(2)}) async-start(), calls=%async_computation.2 | async-start | bytes 16515072 | tf_op jit(solution)/shard_map/all_gather | solution.py:148
  292.6 238.7 %reduce-scatter.2.cloned.1.call-start = ((), (), s32[]{:S(2)}) async-start(), calls=%async_computation.4 | async-start | bytes 1310720 | tf_op jit(solution)/shard_map/reduce_scatter | solution.py:158
Sparse Core Ops, SparseCore 0:
  234.4 28.8 all-gather.11
  291.4 31.0 all-gather.5
  324.4 81.8 all-gather.9
  408.1 80.9 all-gather.7
  506.4 24.8 reduce-scatter.1
where the time goes:
time: 546 us; the launch traced here: 540 us
  waiting for transfers between devices  224 us (41%)
  matrix products  163 us (30%)
  other arithmetic  71.6 us (13%)
  local copies, waits for them, and re-layouts  49.5 us (9%)
  blocking collectives  17.2 us (3%)
  between operations  13.4 us (2%)
    dot_general x2, matrix products, lookup_payload_outer(): jnp.einsum('thk,tshk,shk->tsh', acceptance_product, factor, key, precisio...  132 us
    all_gather x1, waiting for transfers between devices, local(): lax.all_gather(feedforward_output_matrix, 'seq', axis=0, tiled=True)  83.8 us
    all_gather x1, waiting for transfers between devices, local(): lax.all_gather(feedforward_query_matrix, 'seq', axis=0, tiled=True)  82.8 us
    all_gather x1, waiting for transfers between devices, local(): whole = lax.all_gather(xk, 'hid', axis=1, tiled=True)  29.9 us
    dynamic_update_slice x4, local copies, waits for them, and re-layouts, local(): local_state, pieces = lax.scan(step, zero_state, blocks)  27.4 us
    reduce_scatter x1, waiting for transfers between devices, local(): lax.psum_scatter(down.astype(jnp.bfloat16), 'hid', scatter_dimension=1, t...  25 us
    another operation x1, other arithmetic, local(): preceding_rows = jnp.cumsum(logw_rows, axis=0) - logw_rows  23.9 us
    dot_general x2, other arithmetic, lookup_payload_outer(): jnp.einsum('thk,tshk,shk->tsh', acceptance_product, factor, key, precisio...  22.7 us
  transfers between devices with their start and end apart: 6, of which 5 were waited for; matrix products, arithmetic and copies ran while one was open for 5% of the time, Pallas kernels for 0%

commit v1 on v0

v1 whole, which is shorter than its diff:
```python
import functools

import jax
import jax.numpy as jnp
from jax import lax
from jax.experimental import pallas as pl
from jax.experimental.pallas import tpu as pltpu
from jax.sharding import PartitionSpec as P

EPS_GROUP = 0.00064
EPS_LAYER = 1e-05
EXACT = lax.Precision.HIGHEST
F32 = jnp.float32
BF16 = jnp.bfloat16
LANES = 128
TAIL = 16


def dot(a, b, dims=((1,), (0,)), precision=None):
    return lax.dot_general(
        a, b, (dims, ((), ())), precision=precision, preferred_element_type=F32
    )


def iota(shape, axis):
    return lax.broadcasted_iota(jnp.int32, shape, axis)


def block_kernel(
    n_seq,
    n_hid,
    head,
    skip_ref,
    r_ref,
    k_ref,
    v_ref,
    gate_ref,
    logit_ref,
    boost_ref,
    gscale_ref,
    goffset_ref,
    nscale_ref,
    noffset_ref,
    blend_ref,
    w1_ref,
    w2_ref,
    out_ref,
    states,
    wkv,
    rdec,
    rmid,
    kmid,
    kend,
    middle,
    stats,
    edge_out,
    edge_in,
    xk,
    xa,
    w1g,
    w2g,
    part_out,
    part_in,
    hidden,
    down_out,
    down_in,
    sa_send,
    sa_recv,
    sb_send,
    sb_recv,
    st_send,
    st_recv,
    edge_send,
    edge_recv,
    w_send,
    w_recv,
    w_local,
    a_send,
    a_recv,
    b_send,
    b_recv,
    c_send,
    c_recv,
    d_send,
    d_recv,
):
    rows, width = skip_ref.shape
    depth, units = w1_ref.shape
    q = n_seq // n_hid
    pairs = width // LANES
    s = lax.axis_index("seq")
    h = lax.axis_index("hid")
    g = lax.div(s, q)
    j = lax.rem(s, q)

    def at(seq, hid):
        return {"seq": seq, "hid": hid}

    def copy(src, dst, send, recv, seq, hid):
        return pltpu.make_async_remote_copy(
            src_ref=src,
            dst_ref=dst,
            send_sem=send,
            recv_sem=recv,
            device_id=at(seq, hid),
            device_id_type=pl.DeviceIdType.MESH,
        )

    def ring(base, i, size):
        return lax.rem(base + i, size)

    def loop(start, stop, body):
        def step(i, carry):
            body(i)
            return carry

        lax.fori_loop(start, stop, step, 0)

    barrier = pltpu.get_barrier_semaphore()

    def greet(seq, hid):
        pl.semaphore_signal(
            barrier, inc=1, device_id=at(seq, hid), device_id_type=pl.DeviceIdType.MESH
        )

    loop(1, n_seq, lambda i: greet(ring(s, i, n_seq), h))
    loop(1, n_hid, lambda i: greet(s, ring(h, i, n_hid)))

    def greet_cross(i):
        z = ring(h, i, n_hid)

        @pl.when(jnp.logical_or(z != h, g != h))
        def _():
            greet(h * q + j, z)

        far = ring(g, i, n_hid)

        @pl.when(jnp.logical_or(far != g, g != h))
        def _():
            greet(far * q + j, g)

    loop(0, n_hid, greet_cross)

    logw = -jnp.exp(logit_ref[...])
    tri = (iota((rows, rows), 0) >= iota((rows, rows), 1)).astype(F32)
    inclusive = dot(tri, logw, precision=EXACT)
    exclusive = inclusive - logw
    centre_row = inclusive[rows // 2 - 1 : rows // 2]
    total = inclusive[rows - 1 : rows]
    r_all = r_ref[...].astype(F32)
    k_all = k_ref[...].astype(F32)
    rdec[...] = r_all * jnp.exp(exclusive)
    rmid[...] = r_all * jnp.exp(exclusive - centre_row)
    kmid[...] = (k_all * jnp.exp(centre_row - inclusive)).astype(BF16)
    kend[...] = (k_all * jnp.exp(total - inclusive)).astype(BF16)
    decay = jnp.exp(total)
    decay_high = decay.astype(BF16).astype(F32)
    tail_row = iota((TAIL, width), 0)
    states[s, head : head + TAIL, :] = jnp.where(
        tail_row == 0, decay_high, jnp.where(tail_row == 1, decay - decay_high, 0.0)
    ).astype(BF16)

    low = iota((rows, LANES), 1) < head
    low_state = iota((head, LANES), 1) < head
    strict = iota((rows, rows), 0) > iota((rows, rows), 1)
    same = (iota((LANES, LANES), 0) < head) == (iota((LANES, LANES), 1) < head)
    same_head = same.astype(F32)

    def at_pair(p):
        return pl.ds(pl.multiple_of(p * LANES, LANES), LANES)

    def chunk(p):
        cols = at_pair(p)
        rm = rmid[:, cols]
        km = kmid[:, cols]
        vv = v_ref[:, cols]
        vf = vv.astype(F32)
        first = dot(jnp.where(low, rm, 0.0).astype(BF16), km, ((1,), (1,)))
        second = dot(jnp.where(low, 0.0, rm).astype(BF16), km, ((1,), (1,)))
        first = jnp.where(strict, first, 0.0).astype(BF16)
        second = jnp.where(strict, second, 0.0).astype(BF16)
        own = r_ref[:, cols].astype(F32) * boost_ref[:, cols] * k_ref[:, cols].astype(F32)
        wkv[:, cols] = (
            dot(first, jnp.where(low, vf, 0.0).astype(BF16))
            + dot(second, jnp.where(low, 0.0, vf).astype(BF16))
            + dot(own, same_head, precision=EXACT) * vf
        )
        outer = dot(kend[:, cols], vv, ((0,), (0,)))
        states[s, 0:head, cols] = jnp.where(
            low_state, outer[0:head], outer[head : 2 * head]
        ).astype(BF16)

    loop(0, pairs, chunk)

    self_cross = jnp.where(g == h, 1, 0)
    pl.semaphore_wait(barrier, (n_seq - 1) + (n_hid - 1) + 2 * (n_hid - self_cross))

    def send_state(i):
        peer = ring(g, i, n_hid) * q + j
        return copy(states.at[s], states.at[s], sa_send.at[i], sa_recv.at[i], peer, h)

    def recv_state(i):
        slot = ring(g + n_hid, -i, n_hid) * q + j
        return copy(states.at[slot], states.at[slot], sa_send.at[i], sa_recv.at[i], s, h)

    def pass_state(e, i):
        slot = ring(g + n_hid, -i, n_hid) * q + j
        peer = g * q + ring(j, e, q)
        n = (e - 1) * n_hid + i
        return copy(states.at[slot], states.at[slot], sb_send.at[n], sb_recv.at[n], peer, h)

    def take_state(e, i):
        slot = ring(g + n_hid, -i, n_hid) * q + ring(j + q, -e, q)
        n = (e - 1) * n_hid + i
        return copy(states.at[slot], states.at[slot], sb_send.at[n], sb_recv.at[n], s, h)

    loop(1, n_hid, lambda i: send_state(i).start())

    def relay(i):
        @pl.when(i > 0)
        def _():
            recv_state(i).wait_recv()

        for e in range(1, q):
            pass_state(e, i).start()

    loop(0, n_hid, relay)

    def send_weight(e):
        peer = g * q + ring(j, e, q)
        return (
            copy(w1_ref, w1g.at[j], w_send.at[0, e], w_recv.at[0, e], peer, h),
            copy(w2_ref, w2g.at[j], w_send.at[1, e], w_recv.at[1, e], peer, h),
        )

    def take_weight(e):
        slot = ring(j + q, -e, q)
        return (
            copy(w1_ref, w1g.at[slot], w_send.at[0, e], w_recv.at[0, e], s, h),
            copy(w2_ref, w2g.at[slot], w_send.at[1, e], w_recv.at[1, e], s, h),
        )

    keep1 = pltpu.make_async_copy(w1_ref, w1g.at[j], w_local.at[0])
    keep2 = pltpu.make_async_copy(w2_ref, w2g.at[j], w_local.at[1])
    keep1.start()
    keep2.start()
    for e in range(1, q):
        for c in send_weight(e):
            c.start()

    for e in range(1, q):
        loop(0, n_hid, lambda i: take_state(e, i).wait_recv())

    def earlier(i, weight):
        b = n_seq - 1 - i
        valid = b < s
        tail = states[b, head : head + TAIL, :].astype(F32)
        step = tail[0:1] + tail[1:2]
        now = jnp.where(valid, weight, 0.0)
        for p in range(pairs):
            cols = slice(p * LANES, (p + 1) * LANES)
            packed = states[b, 0:head, cols].astype(F32)
            full = jnp.concatenate(
                [jnp.where(low_state, packed, 0.0), jnp.where(low_state, 0.0, packed)], axis=0
            ).astype(BF16)
            wkv[:, cols] += dot((rdec[:, cols] * now[:, cols]).astype(BF16), full)
        return jnp.where(valid, weight * step, weight)

    lax.fori_loop(0, n_seq, earlier, jnp.ones((1, width), F32))

    def finish(p, carry):
        first, second = carry
        cols = at_pair(p)
        x = wkv[:, cols]
        c = x - dot(x, same_head, precision=EXACT) * (1.0 / head)
        spread = dot(c * c, same_head, precision=EXACT) * (1.0 / head)
        n = c * lax.rsqrt(spread + EPS_GROUP) * gscale_ref[:, cols] + goffset_ref[:, cols]
        gate = gate_ref[:, cols].astype(F32)
        m = skip_ref[:, cols].astype(F32) + n * (gate / (1.0 + jnp.exp(-gate)))
        middle[:, cols] = m
        return (
            first + jnp.sum(m, axis=1, keepdims=True),
            second + jnp.sum(m * m, axis=1, keepdims=True),
        )

    zero = jnp.zeros((rows, 1), F32)
    first, second = lax.fori_loop(0, pairs, finish, (zero, zero))

    lane = iota((rows, LANES), 1)
    table = jnp.where(lane == 0, first, jnp.where(lane == 1, second, 0.0))
    stats[h] = table.T[0:8]

    def send_stat(i):
        z = ring(h, i, n_hid)
        return copy(stats.at[h], stats.at[h], st_send.at[i], st_recv.at[i], s, z)

    def take_stat(i):
        z = ring(h + n_hid, -i, n_hid)
        return copy(stats.at[z], stats.at[z], st_send.at[i], st_recv.at[i], s, h)

    loop(1, n_hid, lambda i: send_stat(i).start())
    loop(1, n_hid, lambda i: take_stat(i).wait_recv())
    sums = lax.fori_loop(0, n_hid, lambda z, a: a + stats[z], jnp.zeros((8, rows), F32))
    sums = jnp.concatenate([sums, jnp.zeros((LANES - 8, rows), F32)], axis=0).T
    full_width = width * n_hid
    mean = sums[:, 0:1] / full_width
    var = sums[:, 1:2] / full_width - mean * mean
    xn = (
        (middle[...] - mean) * lax.rsqrt(var + EPS_LAYER) * nscale_ref[...] + noffset_ref[...]
    ).astype(BF16)
    edge_out[...] = xn[rows - TAIL : rows]
    to_next = copy(edge_out, edge_in, edge_send, edge_recv, ring(s, 1, n_seq), h)

    @pl.when(s < n_seq - 1)
    def _():
        to_next.start()

    @pl.when(s == 0)
    def _():
        edge_in[...] = jnp.zeros_like(edge_in)

    @pl.when(s > 0)
    def _():
        to_next.wait_recv()

    wide = xn.astype(F32)
    carried = edge_in[...].astype(F32)[TAIL - 1 : TAIL]
    prev = jnp.where(iota((rows, width), 0) == 0, carried, pltpu.roll(wide, 1, 0))
    xk[...] = (wide + (prev - wide) * blend_ref[...]).astype(BF16)

    def send_a(i):
        return copy(
            xk, xa.at[g], a_send.at[i], a_recv.at[g], h * q + j, ring(h, i, n_hid)
        )

    def take_a(far):
        return copy(xk, xa.at[far], a_send.at[0], a_recv.at[far], s, h)

    def foreign(i):
        return jnp.logical_or(i != 0, g != h)

    def start_a(i):
        @pl.when(foreign(i))
        def _():
            send_a(i).start()

    @pl.when(g == h)
    def _():
        xa[g] = xk[...]

    loop(0, n_hid, start_a)

    keep1.wait()
    keep2.wait()
    for e in range(1, q):
        for c in take_weight(e):
            c.wait_recv()

    tile = 256 if units % 256 == 0 else units

    def partial_b(far):
        def column(c):
            cols = pl.ds(pl.multiple_of(c * tile, tile), tile) if tile < units else slice(None)
            total_tile = dot(xa[far, :, 0:depth], w1g[0, :, cols])
            for e in range(1, q):
                total_tile += dot(xa[far, :, e * depth : (e + 1) * depth], w1g[e, :, cols])
            part_out[far, :, cols] = total_tile.astype(BF16)

        loop(0, units // tile, column)

    def send_b(far):
        return copy(
            part_out.at[far], part_in.at[g], b_send.at[far], b_recv.at[g], far * q + j, h
        )

    def take_b(far):
        return copy(part_out.at[far], part_in.at[far], b_send.at[far], b_recv.at[far], s, h)

    def phase_b(i):
        far = ring(g, i + 1, n_hid)

        @pl.when(jnp.logical_or(far != g, g != h))
        def _():
            take_a(far).wait_recv()

        partial_b(far)

        @pl.when(far != g)
        def _():
            send_b(far).start()

    loop(0, n_hid, phase_b)
    loop(1, n_hid, lambda i: take_b(ring(g, i, n_hid)).wait_recv())

    def activate(c):
        cols = pl.ds(pl.multiple_of(c * tile, tile), tile) if tile < units else slice(None)
        pre = lax.fori_loop(
            1,
            n_hid,
            lambda i, a: a + part_in[ring(g, i, n_hid), :, cols].astype(F32),
            part_out[g, :, cols].astype(F32),
        )
        hidden[g, :, cols] = jnp.square(jnp.maximum(pre, 0.0)).astype(BF16)

    loop(0, units // tile, activate)

    def send_c(far):
        return copy(hidden.at[g], hidden.at[g], c_send.at[far], c_recv.at[g], far * q + j, h)

    def take_c(far):
        return copy(hidden.at[far], hidden.at[far], c_send.at[far], c_recv.at[far], s, h)

    loop(1, n_hid, lambda i: send_c(ring(g, i, n_hid)).start())

    depth_tile = 256 if depth % 256 == 0 else depth

    def partial_d(far):
        for e in range(q):
            for c in range(depth // depth_tile):
                lo = c * depth_tile
                col = e * depth + lo
                down_out[far, :, col : col + depth_tile] = dot(
                    hidden[far], w2g[e, lo : lo + depth_tile, :], ((1,), (1,))
                ).astype(BF16)

    def send_d(far):
        return copy(
            down_out.at[far], down_in.at[h], d_send.at[far], d_recv.at[h], far * q + j, g
        )

    def take_d(z):
        return copy(down_out.at[z], down_in.at[z], d_send.at[z], d_recv.at[z], s, h)

    def phase_d(i):
        far = ring(g, i, n_hid)

        @pl.when(i > 0)
        def _():
            take_c(far).wait_recv()

        partial_d(far)

        @pl.when(foreign(i))
        def _():
            send_d(far).start()

        @pl.when(jnp.logical_not(foreign(i)))
        def _():
            down_in[h] = down_out[far]

    loop(0, n_hid, phase_d)

    def end_d(z):
        @pl.when(jnp.logical_or(z != h, g != h))
        def _():
            take_d(z).wait_recv()

    loop(0, n_hid, end_d)

    def result(p):
        cols = at_pair(p)
        down = lax.fori_loop(
            0,
            n_hid,
            lambda z, a: a + down_in[z, :, cols].astype(F32),
            jnp.zeros((rows, LANES), F32),
        )
        out_ref[:, cols] = (middle[:, cols] + down).astype(BF16)

    loop(0, pairs, result)

    loop(1, n_hid, lambda i: send_state(i).wait_send())
    for e in range(1, q):
        loop(0, n_hid, lambda i: pass_state(e, i).wait_send())
        for c in send_weight(e):
            c.wait_send()
    loop(1, n_hid, lambda i: send_stat(i).wait_send())

    @pl.when(s < n_seq - 1)
    def _():
        to_next.wait_send()

    def end_sends(i):
        far = ring(g, i, n_hid)

        @pl.when(foreign(i))
        def _():
            send_a(i).wait_send()
            send_d(far).wait_send()

        @pl.when(i > 0)
        def _():
            send_b(far).wait_send()
            send_c(far).wait_send()

    loop(0, n_hid, end_sends)


def local(n_seq, n_hid, *args):
    skip = args[0]
    boost = args[6]
    w1 = args[12]
    rows, width = skip.shape
    heads, head = boost.shape
    depth, units = w1.shape
    q = n_seq // n_hid
    vmem = pl.BlockSpec(memory_space=pltpu.VMEM)
    anywhere = pl.BlockSpec(memory_space=pl.ANY)
    dma = pltpu.SemaphoreType.DMA
    operands = list(args[:6]) + [a.reshape(1, width) for a in args[6:12]] + list(args[12:])
    return pl.pallas_call(
        functools.partial(block_kernel, n_seq, n_hid, head),
        out_shape=jax.ShapeDtypeStruct((rows, width), BF16),
        in_specs=[vmem] * 12 + [anywhere] * 2,
        out_specs=vmem,
        scratch_shapes=[
            pltpu.VMEM((n_seq, head + TAIL, width), BF16),
            pltpu.VMEM((rows, width), F32),
            pltpu.VMEM((rows, width), F32),
            pltpu.VMEM((rows, width), F32),
            pltpu.VMEM((rows, width), BF16),
            pltpu.VMEM((rows, width), BF16),
            pltpu.VMEM((rows, width), F32),
            pltpu.VMEM((n_hid, 8, rows), F32),
            pltpu.VMEM((TAIL, width), BF16),
            pltpu.VMEM((TAIL, width), BF16),
            pltpu.VMEM((rows, width), BF16),
            pltpu.VMEM((n_hid, rows, width), BF16),
            pltpu.VMEM((q, depth, units), BF16),
            pltpu.VMEM((q, depth, units), BF16),
            pltpu.VMEM((n_hid, rows, units), BF16),
            pltpu.VMEM((n_hid, rows, units), BF16),
            pltpu.VMEM((n_hid, rows, units), BF16),
            pltpu.VMEM((n_hid, rows, width), BF16),
            pltpu.VMEM((n_hid, rows, width), BF16),
            dma((n_hid,)),
            dma((n_hid,)),
            dma((q * n_hid,)),
            dma((q * n_hid,)),
            dma((n_hid,)),
            dma((n_hid,)),
            dma,
            dma,
            dma((2, q)),
            dma((2, q)),
            dma((2,)),
            dma((n_hid,)),
            dma((n_hid,)),
            dma((n_hid,)),
            dma((n_hid,)),
            dma((n_hid,)),
            dma((n_hid,)),
            dma((n_hid,)),
            dma((n_hid,)),
        ],
        compiler_params=pltpu.CompilerParams(
            collective_id=0, has_side_effects=True, vmem_limit_bytes=48 * 2**20
        ),
    )(*operands)


def solution(mesh):
    return jax.shard_map(
        functools.partial(local, mesh.shape["seq"], mesh.shape["hid"]),
        mesh=mesh,
        in_specs=(P("seq", "hid"),) * 6
        + (P("hid", None),)
        + (P("hid"),) * 5
        + (P("seq", "hid"),) * 2,
        out_specs=P("seq", "hid"),
        check_vma=False,
    )
```

time: 546 us -> 160 us (0.29)
  the two profiles are of different devices: /device:TPU:24 before, /device:TPU:7 now
where the time goes in v1:
time: 160 us; the launch traced here: 159 us
  Pallas kernels  146 us (91%)
  local copies, waits for them, and re-layouts  13.7 us (9%)
    pallas_call x1, Pallas kernels, local(): pl.pallas_call(functools.partial(block_kernel, n_seq, n_hid, head), out_s...  146 us
    unnamed x27, local copies, waits for them, and re-layouts  12.9 us

profile of v1, /device:TPU:7, one launch (start us, length us, event | category | flops | bytes accessed | tf_op | source)
XLA Modules:
  0.0 159.5 jit_solution(12686645084698923017)
XLA Ops:
  0.0 0.8 reshape.18.boost_ref
  0.8 0.0 copy-start
  0.8 1.5 copy-done
  2.3 0.0 copy-start.1
  2.3 1.5 copy-done.1
  3.8 0.0 copy-start.2
  3.8 1.0 copy-done.2
  4.8 0.0 copy-start.3
  4.8 0.9 copy-done.3
  5.8 0.0 copy-start.4
  5.8 0.9 copy-done.4
  6.7 0.0 copy-start.5
  6.7 0.9 copy-done.5
  7.7 0.0 copy-start.6
  7.7 0.9 copy-done.6
  8.6 0.0 copy-start.7
  8.6 0.9 copy-done.7
  9.6 0.7 copy-done.8
  10.3 0.7 copy-done.9
  10.9 0.7 copy-done.10
  11.6 0.7 copy-done.11
  12.3 0.7 copy-done.12
  13.0 145.8 %shard_map.136 = bf16[128,1024]{1,0:T(8,128)(2,1)S(1)} custom-call(bf16[128,1024]{1,0:T(8,128)(2,1)S(1)} %copy-done.3, bf16[128,1024]{1,0:T(8,128)(2,1)S(1)} %copy-done.4, bf16[128,1024]{1,0:T(8,128)(2,1)S(1)} %copy-done.5, bf16[128,1024]{1,0:T(8,128)(2,1)S(1)} %copy-done.6, bf16[128,1024]{1,0:T(8,128)(2,1)S(1)} %copy-done.7, f32[128,1024]{1,0:T(8,128)S(1)} %copy-done.2, ...), custom_call_target="tpu_custom_call" | custom-call | tf_op jit(solution)/shard_map/pallas_call | solution.py:511
  158.8 0.7 copy.16
  (5 shorter events, 0.0 us)
Async XLA Ops:
  0.8 1.5 copy-start
  2.3 1.5 copy-start.1
  3.8 1.0 copy-start.2
  4.8 0.9 copy-start.3
  5.8 0.9 copy-start.4
  6.7 0.9 copy-start.5
  7.7 0.9 copy-start.6
  8.6 0.9 copy-start.7
  9.6 0.7 copy-start.8
  10.3 0.7 copy-start.9
  10.9 0.7 copy-start.10
  11.6 0.7 copy-start.11
  12.3 0.7 copy-start.12

commit v2 on v1

--- a/solution.py
+++ b/solution.py
@@ -9,27 +9,49 @@
 
 EPS_GROUP = 0.00064
 EPS_LAYER = 1e-05
-EXACT = lax.Precision.HIGHEST
 F32 = jnp.float32
 BF16 = jnp.bfloat16
 LANES = 128
 TAIL = 16
 
 
-def dot(a, b, dims=((1,), (0,)), precision=None):
-    return lax.dot_general(
-        a, b, (dims, ((), ())), precision=precision, preferred_element_type=F32
-    )
+def dot(a, b, dims=((1,), (0,))):
+    return lax.dot_general(a, b, (dims, ((), ())), preferred_element_type=F32)
 
 
 def iota(shape, axis):
     return lax.broadcasted_iota(jnp.int32, shape, axis)
+
+
+def halves(x):
+    high = x.astype(BF16)
+    return high, x - high.astype(F32)
+
+
+def head_sums(x, same_head):
+    high, rest = halves(x)
+    return dot(high, same_head) + dot(rest.astype(BF16), same_head)
 
 
 def block_kernel(
     n_seq,
     n_hid,
     head,
+    skip_hbm,
+    r_hbm,
+    k_hbm,
+    v_hbm,
+    gate_hbm,
+    logit_hbm,
+    boost_hbm,
+    gscale_hbm,
+    goffset_hbm,
+    nscale_hbm,
+    noffset_hbm,
+    blend_hbm,
+    w1_ref,
+    w2_ref,
+    out_ref,
     skip_ref,
     r_ref,
     k_ref,
@@ -42,9 +64,7 @@
     nscale_ref,
     noffset_ref,
     blend_ref,
-    w1_ref,
-    w2_ref,
-    out_ref,
+    in_sems,
     states,
     wkv,
     rdec,
@@ -55,7 +75,9 @@
     stats,
     edge_out,
     edge_in,
+    reach,
     xk,
+    planes,
     xa,
     w1g,
     w2g,
@@ -63,6 +85,7 @@
     part_in,
     hidden,
     down_out,
+    down_mid,
     down_in,
     sa_send,
     sa_recv,
@@ -75,6 +98,8 @@
     w_send,
     w_recv,
     w_local,
+    z_send,
+    z_recv,
     a_send,
     a_recv,
     b_send,
@@ -83,6 +108,8 @@
     c_recv,
     d_send,
     d_recv,
+    y_send,
+    y_recv,
 ):
     rows, width = skip_ref.shape
     depth, units = w1_ref.shape
@@ -116,6 +143,32 @@
 
         lax.fori_loop(start, stop, step, 0)
 
+    arrivals = [
+        pltpu.make_async_copy(source, target, in_sems.at[n])
+        for n, (source, target) in enumerate(
+            (
+                (skip_hbm, skip_ref),
+                (r_hbm, r_ref),
+                (k_hbm, k_ref),
+                (v_hbm, v_ref),
+                (gate_hbm, gate_ref),
+                (logit_hbm, logit_ref),
+                (boost_hbm, boost_ref),
+                (gscale_hbm, gscale_ref),
+                (goffset_hbm, goffset_ref),
+                (nscale_hbm, nscale_ref),
+                (noffset_hbm, noffset_ref),
+                (blend_hbm, blend_ref),
+            )
+        )
+    ]
+    for c in arrivals:
+        c.start()
+    keep1 = pltpu.make_async_copy(w1_ref, w1g.at[j], w_local.at[0])
+    keep2 = pltpu.make_async_copy(w2_ref, w2g.at[j], w_local.at[1])
+    keep1.start()
+    keep2.start()
+
     barrier = pltpu.get_barrier_semaphore()
 
     def greet(seq, hid):
@@ -126,24 +179,14 @@
     loop(1, n_seq, lambda i: greet(ring(s, i, n_seq), h))
     loop(1, n_hid, lambda i: greet(s, ring(h, i, n_hid)))
 
-    def greet_cross(i):
-        z = ring(h, i, n_hid)
-
-        @pl.when(jnp.logical_or(z != h, g != h))
-        def _():
-            greet(h * q + j, z)
-
-        far = ring(g, i, n_hid)
-
-        @pl.when(jnp.logical_or(far != g, g != h))
-        def _():
-            greet(far * q + j, g)
-
-    loop(0, n_hid, greet_cross)
+    for c in arrivals:
+        c.wait()
 
     logw = -jnp.exp(logit_ref[...])
-    tri = (iota((rows, rows), 0) >= iota((rows, rows), 1)).astype(F32)
-    inclusive = dot(tri, logw, precision=EXACT)
+    tri = (iota((rows, rows), 0) >= iota((rows, rows), 1)).astype(F32).astype(BF16)
+    top, rest = halves(logw)
+    mid, rest = halves(rest)
+    inclusive = dot(tri, top) + (dot(tri, mid) + dot(tri, rest.astype(BF16)))
     exclusive = inclusive - logw
     centre_row = inclusive[rows // 2 - 1 : rows // 2]
     total = inclusive[rows - 1 : rows]
@@ -164,7 +207,7 @@
     low_state = iota((head, LANES), 1) < head
     strict = iota((rows, rows), 0) > iota((rows, rows), 1)
     same = (iota((LANES, LANES), 0) < head) == (iota((LANES, LANES), 1) < head)
-    same_head = same.astype(F32)
+    same_head = same.astype(F32).astype(BF16)
 
     def at_pair(p):
         return pl.ds(pl.multiple_of(p * LANES, LANES), LANES)
@@ -183,17 +226,22 @@
         wkv[:, cols] = (
             dot(first, jnp.where(low, vf, 0.0).astype(BF16))
             + dot(second, jnp.where(low, 0.0, vf).astype(BF16))
-            + dot(own, same_head, precision=EXACT) * vf
+            + head_sums(own, same_head) * vf
         )
         outer = dot(kend[:, cols], vv, ((0,), (0,)))
         states[s, 0:head, cols] = jnp.where(
             low_state, outer[0:head], outer[head : 2 * head]
         ).astype(BF16)
 
-    loop(0, pairs, chunk)
-
-    self_cross = jnp.where(g == h, 1, 0)
-    pl.semaphore_wait(barrier, (n_seq - 1) + (n_hid - 1) + 2 * (n_hid - self_cross))
+    several = max(n for n in (1, 2, 4) if pairs % n == 0)
+
+    def chunks(i):
+        for n in range(several):
+            chunk(i * several + n)
+
+    loop(0, pairs // several, chunks)
+
+    pl.semaphore_wait(barrier, (n_seq - 1) + (n_hid - 1))
 
     def send_state(i):
         peer = ring(g, i, n_hid) * q + j
@@ -240,10 +288,6 @@
             copy(w2_ref, w2g.at[slot], w_send.at[1, e], w_recv.at[1, e], s, h),
         )
 
-    keep1 = pltpu.make_async_copy(w1_ref, w1g.at[j], w_local.at[0])
-    keep2 = pltpu.make_async_copy(w2_ref, w2g.at[j], w_local.at[1])
-    keep1.start()
-    keep2.start()
     for e in range(1, q):
         for c in send_weight(e):
             c.start()
@@ -251,29 +295,40 @@
     for e in range(1, q):
         loop(0, n_hid, lambda i: take_state(e, i).wait_recv())
 
-    def earlier(i, weight):
-        b = n_seq - 1 - i
+    weight = jnp.ones((1, width), F32)
+    for b in reversed(range(n_seq)):
         valid = b < s
         tail = states[b, head : head + TAIL, :].astype(F32)
-        step = tail[0:1] + tail[1:2]
-        now = jnp.where(valid, weight, 0.0)
-        for p in range(pairs):
-            cols = slice(p * LANES, (p + 1) * LANES)
-            packed = states[b, 0:head, cols].astype(F32)
-            full = jnp.concatenate(
-                [jnp.where(low_state, packed, 0.0), jnp.where(low_state, 0.0, packed)], axis=0
-            ).astype(BF16)
-            wkv[:, cols] += dot((rdec[:, cols] * now[:, cols]).astype(BF16), full)
-        return jnp.where(valid, weight * step, weight)
-
-    lax.fori_loop(0, n_seq, earlier, jnp.ones((1, width), F32))
+        reach[b : b + 1, :] = jnp.where(valid, weight, 0.0)
+        weight = jnp.where(valid, weight * (tail[0:1] + tail[1:2]), weight)
+
+    def earlier(p):
+        cols = at_pair(p)
+        rd = rdec[:, cols]
+        total = wkv[:, cols]
+        for start in range(0, n_seq, n_hid):
+            left = []
+            right = []
+            for b in range(start, start + n_hid):
+                packed = states[b, 0:head, cols].astype(F32)
+                right.append(jnp.where(low_state, packed, 0.0).astype(BF16))
+                right.append(jnp.where(low_state, 0.0, packed).astype(BF16))
+                left.append((rd * reach[b : b + 1, cols]).astype(BF16))
+            total += dot(jnp.concatenate(left, axis=1), jnp.concatenate(right, axis=0))
+        wkv[:, cols] = total
+
+    def earliers(i):
+        for n in range(several):
+            earlier(i * several + n)
+
+    loop(0, pairs // several, earliers)
 
     def finish(p, carry):
         first, second = carry
         cols = at_pair(p)
         x = wkv[:, cols]
-        c = x - dot(x, same_head, precision=EXACT) * (1.0 / head)
-        spread = dot(c * c, same_head, precision=EXACT) * (1.0 / head)
+        c = x - head_sums(x, same_head) * (1.0 / head)
+        spread = head_sums(c * c, same_head) * (1.0 / head)
         n = c * lax.rsqrt(spread + EPS_GROUP) * gscale_ref[:, cols] + goffset_ref[:, cols]
         gate = gate_ref[:, cols].astype(F32)
         m = skip_ref[:, cols].astype(F32) + n * (gate / (1.0 + jnp.exp(-gate)))
@@ -284,7 +339,13 @@
         )
 
     zero = jnp.zeros((rows, 1), F32)
-    first, second = lax.fori_loop(0, pairs, finish, (zero, zero))
+
+    def finishes(i, carry):
+        for n in range(several):
+            carry = finish(i * several + n, carry)
+        return carry
+
+    first, second = lax.fori_loop(0, pairs // several, finishes, (zero, zero))
 
     lane = iota((rows, LANES), 1)
     table = jnp.where(lane == 0, first, jnp.where(lane == 1, second, 0.0))
@@ -328,25 +389,37 @@
     prev = jnp.where(iota((rows, width), 0) == 0, carried, pltpu.roll(wide, 1, 0))
     xk[...] = (wide + (prev - wide) * blend_ref[...]).astype(BF16)
 
-    def send_a(i):
-        return copy(
-            xk, xa.at[g], a_send.at[i], a_recv.at[g], h * q + j, ring(h, i, n_hid)
-        )
+    def send_z(i):
+        z = ring(h, i, n_hid)
+        return copy(xk, planes.at[h], z_send.at[i], z_recv.at[i], s, z)
+
+    def take_z(i):
+        z = ring(h + n_hid, -i, n_hid)
+        return copy(xk, planes.at[z], z_send.at[i], z_recv.at[i], s, h)
+
+    def send_a(far):
+        return copy(planes.at[far], xa.at[g], a_send.at[far], a_recv.at[g], far * q + j, h)
 
     def take_a(far):
-        return copy(xk, xa.at[far], a_send.at[0], a_recv.at[far], s, h)
-
-    def foreign(i):
-        return jnp.logical_or(i != 0, g != h)
+        return copy(planes.at[far], xa.at[far], a_send.at[far], a_recv.at[far], s, h)
+
+    loop(1, n_hid, lambda i: send_z(i).start())
+    planes[h] = xk[...]
 
     def start_a(i):
-        @pl.when(foreign(i))
-        def _():
-            send_a(i).start()
-
-    @pl.when(g == h)
-    def _():
-        xa[g] = xk[...]
+        z = ring(h + n_hid, -i, n_hid)
+
+        @pl.when(i > 0)
+        def _():
+            take_z(i).wait_recv()
+
+        @pl.when(z != g)
+        def _():
+            send_a(z).start()
+
+        @pl.when(z == g)
+        def _():
+            xa[g] = planes[z]
 
     loop(0, n_hid, start_a)
 
@@ -379,7 +452,7 @@
     def phase_b(i):
         far = ring(g, i + 1, n_hid)
 
-        @pl.when(jnp.logical_or(far != g, g != h))
+        @pl.when(far != g)
         def _():
             take_a(far).wait_recv()
 
@@ -425,37 +498,48 @@
 
     def send_d(far):
         return copy(
-            down_out.at[far], down_in.at[h], d_send.at[far], d_recv.at[h], far * q + j, g
-        )
-
-    def take_d(z):
-        return copy(down_out.at[z], down_in.at[z], d_send.at[z], d_recv.at[z], s, h)
+            down_out.at[far], down_mid.at[g], d_send.at[far], d_recv.at[g], far * q + j, h
+        )
+
+    def take_d(far):
+        return copy(
+            down_out.at[far], down_mid.at[far], d_send.at[far], d_recv.at[far], s, h
+        )
+
+    def send_y(far):
+        return copy(down_mid.at[far], down_in.at[h], y_send.at[far], y_recv.at[h], s, far)
+
+    def take_y(z):
+        return copy(down_mid.at[z], down_in.at[z], y_send.at[z], y_recv.at[z], s, h)
+
+    def onward(far):
+        @pl.when(far != h)
+        def _():
+            send_y(far).start()
+
+        @pl.when(far == h)
+        def _():
+            down_in[h] = down_mid[far]
+
+    partial_d(g)
+    down_mid[g] = down_out[g]
+    onward(g)
 
     def phase_d(i):
         far = ring(g, i, n_hid)
-
-        @pl.when(i > 0)
-        def _():
-            take_c(far).wait_recv()
-
+        take_c(far).wait_recv()
         partial_d(far)
-
-        @pl.when(foreign(i))
-        def _():
-            send_d(far).start()
-
-        @pl.when(jnp.logical_not(foreign(i)))
-        def _():
-            down_in[h] = down_out[far]
-
-    loop(0, n_hid, phase_d)
-
-    def end_d(z):
-        @pl.when(jnp.logical_or(z != h, g != h))
-        def _():
-            take_d(z).wait_recv()
-
-    loop(0, n_hid, end_d)
+        send_d(far).start()
+
+    loop(1, n_hid, phase_d)
+
+    def phase_y(i):
+        far = ring(g, i, n_hid)
+        take_d(far).wait_recv()
+        onward(far)
+
+    loop(1, n_hid, phase_y)
+    loop(1, n_hid, lambda i: take_y(ring(h, i, n_hid)).wait_recv())
 
     def result(p):
         cols = at_pair(p)
@@ -483,15 +567,14 @@
     def end_sends(i):
         far = ring(g, i, n_hid)
 
-        @pl.when(foreign(i))
-        def _():
-            send_a(i).wait_send()
-            send_d(far).wait_send()
-
         @pl.when(i > 0)
         def _():
+            send_z(i).wait_send()
+            send_a(far).wait_send()
             send_b(far).wait_send()
             send_c(far).wait_send()
+            send_d(far).wait_send()
+            send_y(ring(h, i, n_hid)).wait_send()
 
     loop(0, n_hid, end_sends)
 
@@ -511,9 +594,11 @@
     return pl.pallas_call(
         functools.partial(block_kernel, n_seq, n_hid, head),
         out_shape=jax.ShapeDtypeStruct((rows, width), BF16),
-        in_specs=[vmem] * 12 + [anywhere] * 2,
+        in_specs=[anywhere] * 14,
         out_specs=vmem,
-        scratch_shapes=[
+        scratch_shapes=[pltpu.VMEM(a.shape, a.dtype) for a in operands[:12]]
+        + [
+            dma((12,)),
             pltpu.VMEM((n_seq, head + TAIL, width), BF16),
             pltpu.VMEM((rows, width), F32),
             pltpu.VMEM((rows, width), F32),
@@ -524,7 +609,9 @@
             pltpu.VMEM((n_hid, 8, rows), F32),
             pltpu.VMEM((TAIL, width), BF16),
             pltpu.VMEM((TAIL, width), BF16),
+            pltpu.VMEM((n_seq, width), F32),
             pltpu.VMEM((rows, width), BF16),
+            pltpu.VMEM((n_hid, rows, width), BF16),
             pltpu.VMEM((n_hid, rows, width), BF16),
             pltpu.VMEM((q, depth, units), BF16),
             pltpu.VMEM((q, depth, units), BF16),
@@ -533,6 +620,7 @@
             pltpu.VMEM((n_hid, rows, units), BF16),
             pltpu.VMEM((n_hid, rows, width), BF16),
             pltpu.VMEM((n_hid, rows, width), BF16),
+            pltpu.VMEM((n_hid, rows, width), BF16),
             dma((n_hid,)),
             dma((n_hid,)),
             dma((q * n_hid,)),
@@ -552,9 +640,13 @@
             dma((n_hid,)),
             dma((n_hid,)),
             dma((n_hid,)),
+            dma((n_hid,)),
+            dma((n_hid,)),
+            dma((n_hid,)),
+            dma((n_hid,)),
         ],
         compiler_params=pltpu.CompilerParams(
-            collective_id=0, has_side_effects=True, vmem_limit_bytes=48 * 2**20
+            collective_id=0, has_side_effects=True, vmem_limit_bytes=60 * 2**20
         ),
     )(*operands)
 

time: 160 us -> 140 us (0.88)
  the two profiles are of different devices: /device:TPU:7 before, /device:TPU:24 now
where the time goes in v2:
time: 140 us; the launch traced here: 138 us
  Pallas kernels  135 us (96%)
  local copies, waits for them, and re-layouts  3.03 us (2%)
    pallas_call x1, Pallas kernels, local(): pl.pallas_call(functools.partial(block_kernel, n_seq, n_hid, head), out_s...  135 us

profile of v2, /device:TPU:24, one launch (start us, length us, event | category | flops | bytes accessed | tf_op | source)
XLA Modules:
  0.0 138.3 jit_solution(12263222911214654898)
XLA Ops:
  0.0 1.4 reshape.18.boost_hbm
  1.4 135.2 %shard_map.136 = bf16[128,1024]{1,0:T(8,128)(2,1)} custom-call(bf16[128,1024]{1,0:T(8,128)(2,1)} %skip_hbm.1, bf16[128,1024]{1,0:T(8,128)(2,1)} %r_hbm.1, bf16[128,1024]{1,0:T(8,128)(2,1)} %k_hbm.1, bf16[128,1024]{1,0:T(8,128)(2,1)} %v_hbm.1, bf16[128,1024]{1,0:T(8,128)(2,1)} %gate_hbm.1, f32[128,1024]{1,0:T(8,128)} %logit_hbm.1, ...), custom_call_target="tpu_custom_call" | custom-call | tf_op jit(solution)/shard_map/pallas_call | solution.py:594
  136.6 1.7 %copy.16 = bf16[128,1024]{1,0:T(8,128)(2,1)} copy(bf16[128,1024]{1,0:T(8,128)(2,1)} %shard_map.136) | data formatting | bytes 524288

commit v3 on v2

--- a/solution.py
+++ b/solution.py
@@ -115,6 +115,7 @@
     depth, units = w1_ref.shape
     q = n_seq // n_hid
     pairs = width // LANES
+    half = rows // 2
     s = lax.axis_index("seq")
     h = lax.axis_index("hid")
     g = lax.div(s, q)
@@ -389,169 +390,174 @@
     prev = jnp.where(iota((rows, width), 0) == 0, carried, pltpu.roll(wide, 1, 0))
     xk[...] = (wide + (prev - wide) * blend_ref[...]).astype(BF16)
 
-    def send_z(i):
+    def send_z(c, i):
         z = ring(h, i, n_hid)
-        return copy(xk, planes.at[h], z_send.at[i], z_recv.at[i], s, z)
-
-    def take_z(i):
+        source = xk.at[pl.ds(c * half, half)]
+        return copy(source, planes.at[c, h], z_send.at[c, i], z_recv.at[c, i], s, z)
+
+    def take_z(c, i):
         z = ring(h + n_hid, -i, n_hid)
-        return copy(xk, planes.at[z], z_send.at[i], z_recv.at[i], s, h)
-
-    def send_a(far):
-        return copy(planes.at[far], xa.at[g], a_send.at[far], a_recv.at[g], far * q + j, h)
-
-    def take_a(far):
-        return copy(planes.at[far], xa.at[far], a_send.at[far], a_recv.at[far], s, h)
-
-    loop(1, n_hid, lambda i: send_z(i).start())
-    planes[h] = xk[...]
-
-    def start_a(i):
-        z = ring(h + n_hid, -i, n_hid)
-
-        @pl.when(i > 0)
+        source = xk.at[pl.ds(c * half, half)]
+        return copy(source, planes.at[c, z], z_send.at[c, i], z_recv.at[c, i], s, h)
+
+    def within(source, target, send, recv):
+        def start(c, far):
+            return copy(
+                source.at[c, far], target.at[c, g], send.at[c, far], recv.at[c, g], far * q + j, h
+            )
+
+        def take(c, far):
+            return copy(
+                source.at[c, far], target.at[c, far], send.at[c, far], recv.at[c, far], s, h
+            )
+
+        return start, take
+
+    send_a, take_a = within(planes, xa, a_send, a_recv)
+    send_b, take_b = within(part_out, part_in, b_send, b_recv)
+    send_d, take_d = within(down_out, down_mid, d_send, d_recv)
+
+    for c in range(2):
+        loop(1, n_hid, lambda i: send_z(c, i).start())
+        planes[c, h] = xk[c * half : (c + 1) * half]
+
+    def phase_a(c):
+        def start_a(i):
+            z = ring(h + n_hid, -i, n_hid)
+
+            @pl.when(i > 0)
+            def _():
+                take_z(c, i).wait_recv()
+
+            @pl.when(z != g)
+            def _():
+                send_a(c, z).start()
+
+            @pl.when(z == g)
+            def _():
+                xa[c, g] = planes[c, z]
+
+        loop(0, n_hid, start_a)
+
+    tile = 256 if units % 256 == 0 else units
+    lines = n_hid * half
+
+    def tile_at(n):
+        return pl.ds(pl.multiple_of(n * tile, tile), tile) if tile < units else slice(None)
+
+    def others(body):
+        loop(1, n_hid, lambda i: body(ring(g, i, n_hid)))
+
+    def phase_b(c):
+        others(lambda far: take_a(c, far).wait_recv())
+
+        def column(n):
+            cols = tile_at(n)
+            total_tile = dot(xa[c, :, :, 0:depth].reshape(lines, depth), w1g[0, :, cols])
+            for e in range(1, q):
+                piece = xa[c, :, :, e * depth : (e + 1) * depth].reshape(lines, depth)
+                total_tile += dot(piece, w1g[e, :, cols])
+            part_out[c, :, :, cols] = total_tile.astype(BF16).reshape(n_hid, half, tile)
+
+        loop(0, units // tile, column)
+        others(lambda far: send_b(c, far).start())
+
+    def send_c(c, far):
+        block = hidden.at[c, g]
+        return copy(block, block, c_send.at[c, far], c_recv.at[c, g], far * q + j, h)
+
+    def take_c(c, far):
+        block = hidden.at[c, far]
+        return copy(block, block, c_send.at[c, far], c_recv.at[c, far], s, h)
+
+    def phase_c(c):
+        others(lambda far: take_b(c, far).wait_recv())
+
+        def activate(n):
+            cols = tile_at(n)
+            pre = lax.fori_loop(
+                1,
+                n_hid,
+                lambda i, a: a + part_in[c, ring(g, i, n_hid), :, cols].astype(F32),
+                part_out[c, g, :, cols].astype(F32),
+            )
+            hidden[c, g, :, cols] = jnp.square(jnp.maximum(pre, 0.0)).astype(BF16)
+
+        loop(0, units // tile, activate)
+        others(lambda far: send_c(c, far).start())
+
+    depth_tile = 256 if depth % 256 == 0 else depth
+
+    def send_y(c, far):
+        return copy(
+            down_mid.at[c, far], down_in.at[c, h], y_send.at[c, far], y_recv.at[c, h], s, far
+        )
+
+    def take_y(c, z):
+        return copy(down_mid.at[c, z], down_in.at[c, z], y_send.at[c, z], y_recv.at[c, z], s, h)
+
+    def onward(c, far):
+        @pl.when(far != h)
         def _():
-            take_z(i).wait_recv()
-
-        @pl.when(z != g)
+            send_y(c, far).start()
+
+        @pl.when(far == h)
         def _():
-            send_a(z).start()
-
-        @pl.when(z == g)
-        def _():
-            xa[g] = planes[z]
-
-    loop(0, n_hid, start_a)
-
+            down_in[c, h] = down_mid[c, far]
+
+    def phase_d(c):
+        others(lambda far: take_c(c, far).wait_recv())
+        for e in range(q):
+            for lo in range(0, depth, depth_tile):
+                col = e * depth + lo
+                piece = dot(
+                    hidden[c].reshape(lines, units), w2g[e, lo : lo + depth_tile, :], ((1,), (1,))
+                )
+                down_out[c, :, :, col : col + depth_tile] = piece.astype(BF16).reshape(
+                    n_hid, half, depth_tile
+                )
+        others(lambda far: send_d(c, far).start())
+        down_mid[c, g] = down_out[c, g]
+        onward(c, g)
+
+    def phase_y(c):
+        def step(far):
+            take_d(c, far).wait_recv()
+            onward(c, far)
+
+        others(step)
+
+    phase_a(0)
     keep1.wait()
     keep2.wait()
     for e in range(1, q):
         for c in take_weight(e):
             c.wait_recv()
-
-    tile = 256 if units % 256 == 0 else units
-
-    def partial_b(far):
-        def column(c):
-            cols = pl.ds(pl.multiple_of(c * tile, tile), tile) if tile < units else slice(None)
-            total_tile = dot(xa[far, :, 0:depth], w1g[0, :, cols])
-            for e in range(1, q):
-                total_tile += dot(xa[far, :, e * depth : (e + 1) * depth], w1g[e, :, cols])
-            part_out[far, :, cols] = total_tile.astype(BF16)
-
-        loop(0, units // tile, column)
-
-    def send_b(far):
-        return copy(
-            part_out.at[far], part_in.at[g], b_send.at[far], b_recv.at[g], far * q + j, h
-        )
-
-    def take_b(far):
-        return copy(part_out.at[far], part_in.at[far], b_send.at[far], b_recv.at[far], s, h)
-
-    def phase_b(i):
-        far = ring(g, i + 1, n_hid)
-
-        @pl.when(far != g)
-        def _():
-            take_a(far).wait_recv()
-
-        partial_b(far)
-
-        @pl.when(far != g)
-        def _():
-            send_b(far).start()
-
-    loop(0, n_hid, phase_b)
-    loop(1, n_hid, lambda i: take_b(ring(g, i, n_hid)).wait_recv())
-
-    def activate(c):
-        cols = pl.ds(pl.multiple_of(c * tile, tile), tile) if tile < units else slice(None)
-        pre = lax.fori_loop(
-            1,
-            n_hid,
-            lambda i, a: a + part_in[ring(g, i, n_hid), :, cols].astype(F32),
-            part_out[g, :, cols].astype(F32),
-        )
-        hidden[g, :, cols] = jnp.square(jnp.maximum(pre, 0.0)).astype(BF16)
-
-    loop(0, units // tile, activate)
-
-    def send_c(far):
-        return copy(hidden.at[g], hidden.at[g], c_send.at[far], c_recv.at[g], far * q + j, h)
-
-    def take_c(far):
-        return copy(hidden.at[far], hidden.at[far], c_send.at[far], c_recv.at[far], s, h)
-
-    loop(1, n_hid, lambda i: send_c(ring(g, i, n_hid)).start())
-
-    depth_tile = 256 if depth % 256 == 0 else depth
-
-    def partial_d(far):
-        for e in range(q):
-            for c in range(depth // depth_tile):
-                lo = c * depth_tile
-                col = e * depth + lo
-                down_out[far, :, col : col + depth_tile] = dot(
-                    hidden[far], w2g[e, lo : lo + depth_tile, :], ((1,), (1,))
-                ).astype(BF16)
-
-    def send_d(far):
-        return copy(
-            down_out.at[far], down_mid.at[g], d_send.at[far], d_recv.at[g], far * q + j, h
-        )
-
-    def take_d(far):
-        return copy(
-            down_out.at[far], down_mid.at[far], d_send.at[far], d_recv.at[far], s, h
-        )
-
-    def send_y(far):
-        return copy(down_mid.at[far], down_in.at[h], y_send.at[far], y_recv.at[h], s, far)
-
-    def take_y(z):
-        return copy(down_mid.at[z], down_in.at[z], y_send.at[z], y_recv.at[z], s, h)
-
-    def onward(far):
-        @pl.when(far != h)
-        def _():
-            send_y(far).start()
-
-        @pl.when(far == h)
-        def _():
-            down_in[h] = down_mid[far]
-
-    partial_d(g)
-    down_mid[g] = down_out[g]
-    onward(g)
-
-    def phase_d(i):
-        far = ring(g, i, n_hid)
-        take_c(far).wait_recv()
-        partial_d(far)
-        send_d(far).start()
-
-    loop(1, n_hid, phase_d)
-
-    def phase_y(i):
-        far = ring(g, i, n_hid)
-        take_d(far).wait_recv()
-        onward(far)
-
-    loop(1, n_hid, phase_y)
-    loop(1, n_hid, lambda i: take_y(ring(h, i, n_hid)).wait_recv())
-
-    def result(p):
-        cols = at_pair(p)
-        down = lax.fori_loop(
-            0,
-            n_hid,
-            lambda z, a: a + down_in[z, :, cols].astype(F32),
-            jnp.zeros((rows, LANES), F32),
-        )
-        out_ref[:, cols] = (middle[:, cols] + down).astype(BF16)
-
-    loop(0, pairs, result)
+    phase_b(0)
+    phase_a(1)
+    phase_b(1)
+    phase_c(0)
+    phase_c(1)
+    phase_d(0)
+    phase_d(1)
+    phase_y(0)
+    phase_y(1)
+
+    for c in range(2):
+        loop(1, n_hid, lambda i: take_y(c, ring(h, i, n_hid)).wait_recv())
+        span = slice(c * half, (c + 1) * half)
+
+        def result(p):
+            cols = at_pair(p)
+            down = lax.fori_loop(
+                0,
+                n_hid,
+                lambda z, a: a + down_in[c, z, :, cols].astype(F32),
+                jnp.zeros((half, LANES), F32),
+            )
+            out_ref[span, cols] = (middle[span, cols] + down).astype(BF16)
+
+        loop(0, pairs, result)
 
     loop(1, n_hid, lambda i: send_state(i).wait_send())
     for e in range(1, q):
@@ -566,17 +572,13 @@
 
     def end_sends(i):
         far = ring(g, i, n_hid)
-
-        @pl.when(i > 0)
-        def _():
-            send_z(i).wait_send()
-            send_a(far).wait_send()
-            send_b(far).wait_send()
-            send_c(far).wait_send()
-            send_d(far).wait_send()
-            send_y(ring(h, i, n_hid)).wait_send()
-
-    loop(0, n_hid, end_sends)
+        for c in range(2):
+            send_z(c, i).wait_send()
+            for send in (send_a, send_b, send_c, send_d):
+                send(c, far).wait_send()
+            send_y(c, ring(h, i, n_hid)).wait_send()
+
+    loop(1, n_hid, end_sends)
 
 
 def local(n_seq, n_hid, *args):
@@ -611,16 +613,16 @@
             pltpu.VMEM((TAIL, width), BF16),
             pltpu.VMEM((n_seq, width), F32),
             pltpu.VMEM((rows, width), BF16),
-            pltpu.VMEM((n_hid, rows, width), BF16),
-            pltpu.VMEM((n_hid, rows, width), BF16),
+            pltpu.VMEM((2, n_hid, rows // 2, width), BF16),
+            pltpu.VMEM((2, n_hid, rows // 2, width), BF16),
             pltpu.VMEM((q, depth, units), BF16),
             pltpu.VMEM((q, depth, units), BF16),
-            pltpu.VMEM((n_hid, rows, units), BF16),
-            pltpu.VMEM((n_hid, rows, units), BF16),
-            pltpu.VMEM((n_hid, rows, units), BF16),
-            pltpu.VMEM((n_hid, rows, width), BF16),
-            pltpu.VMEM((n_hid, rows, width), BF16),
-            pltpu.VMEM((n_hid, rows, width), BF16),
+            pltpu.VMEM((2, n_hid, rows // 2, units), BF16),
+            pltpu.VMEM((2, n_hid, rows // 2, units), BF16),
+            pltpu.VMEM((2, n_hid, rows // 2, units), BF16),
+            pltpu.VMEM((2, n_hid, rows // 2, width), BF16),
+            pltpu.VMEM((2, n_hid, rows // 2, width), BF16),
+            pltpu.VMEM((2, n_hid, rows // 2, width), BF16),
             dma((n_hid,)),
             dma((n_hid,)),
             dma((q * n_hid,)),
@@ -632,18 +634,18 @@
             dma((2, q)),
             dma((2, q)),
             dma((2,)),
-            dma((n_hid,)),
-            dma((n_hid,)),
-            dma((n_hid,)),
-            dma((n_hid,)),
-            dma((n_hid,)),
-            dma((n_hid,)),
-            dma((n_hid,)),
-            dma((n_hid,)),
-            dma((n_hid,)),
-            dma((n_hid,)),
-            dma((n_hid,)),
-            dma((n_hid,)),
+            dma((2, n_hid)),
+            dma((2, n_hid)),
+            dma((2, n_hid)),
+            dma((2, n_hid)),
+            dma((2, n_hid)),
+            dma((2, n_hid)),
+            dma((2, n_hid)),
+            dma((2, n_hid)),
+            dma((2, n_hid)),
+            dma((2, n_hid)),
+            dma((2, n_hid)),
+            dma((2, n_hid)),
         ],
         compiler_params=pltpu.CompilerParams(
             collective_id=0, has_side_effects=True, vmem_limit_bytes=60 * 2**20

time: 140 us -> 132 us (0.943); the launches traced: 138 us -> 132 us
  Pallas kernels: 135 us -> 129 us
    pallas_call x1, Pallas kernels: 135 us -> 129 us  [local(): pl.pallas_call(functools.partial(block_kernel, n_seq, n_hid, head), out_s...]
where the time goes in v3:
time: 132 us
  Pallas kernels  129 us (98%)
  local copies, waits for them, and re-layouts  3.03 us (2%)
    pallas_call x1, Pallas kernels, local(): pl.pallas_call(functools.partial(block_kernel, n_seq, n_hid, head), out_s...  129 us

profile of v3, /device:TPU:24, one launch (start us, length us, event | category | flops | bytes accessed | tf_op | source)
XLA Modules:
  0.0 131.8 jit_solution(14156902102268110484)
XLA Ops:
  0.0 1.4 %reshape.18.boost_hbm = f32[1,1024]{1,0:T(1,128)} reshape(f32[16,64]{1,0:T(8,128)} %param.20) | data formatting | bytes 8192 | tf_op jit(solution)/shard_map/reshape | solution.py:595
  1.4 128.8 %shard_map.136 = bf16[128,1024]{1,0:T(8,128)(2,1)} custom-call(bf16[128,1024]{1,0:T(8,128)(2,1)} %skip_hbm.1, bf16[128,1024]{1,0:T(8,128)(2,1)} %r_hbm.1, bf16[128,1024]{1,0:T(8,128)(2,1)} %k_hbm.1, bf16[128,1024]{1,0:T(8,128)(2,1)} %v_hbm.1, bf16[128,1024]{1,0:T(8,128)(2,1)} %gate_hbm.1, f32[128,1024]{1,0:T(8,128)} %logit_hbm.1, ...), custom_call_target="tpu_custom_call" | custom-call | tf_op jit(solution)/shard_map/pallas_call | solution.py:596
  130.1 1.7 %copy.16 = bf16[128,1024]{1,0:T(8,128)(2,1)} copy(bf16[128,1024]{1,0:T(8,128)(2,1)} %shard_map.136) | data formatting | bytes 524288

commit v4 on v3

--- a/solution.py
+++ b/solution.py
@@ -191,11 +191,7 @@
     exclusive = inclusive - logw
     centre_row = inclusive[rows // 2 - 1 : rows // 2]
     total = inclusive[rows - 1 : rows]
-    r_all = r_ref[...].astype(F32)
     k_all = k_ref[...].astype(F32)
-    rdec[...] = r_all * jnp.exp(exclusive)
-    rmid[...] = r_all * jnp.exp(exclusive - centre_row)
-    kmid[...] = (k_all * jnp.exp(centre_row - inclusive)).astype(BF16)
     kend[...] = (k_all * jnp.exp(total - inclusive)).astype(BF16)
     decay = jnp.exp(total)
     decay_high = decay.astype(BF16).astype(F32)
@@ -229,19 +225,24 @@
             + dot(second, jnp.where(low, 0.0, vf).astype(BF16))
             + head_sums(own, same_head) * vf
         )
-        outer = dot(kend[:, cols], vv, ((0,), (0,)))
+    def end_state(p):
+        cols = at_pair(p)
+        outer = dot(kend[:, cols], v_ref[:, cols], ((0,), (0,)))
         states[s, 0:head, cols] = jnp.where(
             low_state, outer[0:head], outer[head : 2 * head]
         ).astype(BF16)
 
     several = max(n for n in (1, 2, 4) if pairs % n == 0)
 
+    def end_states(i):
+        for n in range(several):
+            end_state(i * several + n)
+
     def chunks(i):
         for n in range(several):
             chunk(i * several + n)
 
-    loop(0, pairs // several, chunks)
-
+    loop(0, pairs // several, end_states)
     pl.semaphore_wait(barrier, (n_seq - 1) + (n_hid - 1))
 
     def send_state(i):
@@ -265,15 +266,22 @@
 
     loop(1, n_hid, lambda i: send_state(i).start())
 
+    for e in range(1, q):
+        pass_state(e, 0).start()
+
+    r_all = r_ref[...].astype(F32)
+    rdec[...] = r_all * jnp.exp(exclusive)
+    rmid[...] = r_all * jnp.exp(exclusive - centre_row)
+    kmid[...] = (k_all * jnp.exp(centre_row - inclusive)).astype(BF16)
+    steps = pairs // several
+    loop(0, steps // 2, chunks)
+
     def relay(i):
-        @pl.when(i > 0)
-        def _():
-            recv_state(i).wait_recv()
-
+        recv_state(i).wait_recv()
         for e in range(1, q):
             pass_state(e, i).start()
 
-    loop(0, n_hid, relay)
+    loop(1, n_hid, relay)
 
     def send_weight(e):
         peer = g * q + ring(j, e, q)
@@ -293,6 +301,7 @@
         for c in send_weight(e):
             c.start()
 
+    loop(steps // 2, steps, chunks)
     for e in range(1, q):
         loop(0, n_hid, lambda i: take_state(e, i).wait_recv())
 
@@ -377,18 +386,10 @@
     def _():
         to_next.start()
 
-    @pl.when(s == 0)
-    def _():
-        edge_in[...] = jnp.zeros_like(edge_in)
-
-    @pl.when(s > 0)
-    def _():
-        to_next.wait_recv()
-
     wide = xn.astype(F32)
-    carried = edge_in[...].astype(F32)[TAIL - 1 : TAIL]
-    prev = jnp.where(iota((rows, width), 0) == 0, carried, pltpu.roll(wide, 1, 0))
-    xk[...] = (wide + (prev - wide) * blend_ref[...]).astype(BF16)
+    prev = pltpu.roll(wide, 1, 0)
+    mixed = wide + (prev - wide) * blend_ref[...]
+    xk[half:rows] = mixed[half:rows].astype(BF16)
 
     def send_z(c, i):
         z = ring(h, i, n_hid)
@@ -417,9 +418,24 @@
     send_b, take_b = within(part_out, part_in, b_send, b_recv)
     send_d, take_d = within(down_out, down_mid, d_send, d_recv)
 
-    for c in range(2):
+    def phase_z(c):
         loop(1, n_hid, lambda i: send_z(c, i).start())
         planes[c, h] = xk[c * half : (c + 1) * half]
+
+    phase_z(1)
+
+    @pl.when(s == 0)
+    def _():
+        edge_in[...] = jnp.zeros_like(edge_in)
+
+    @pl.when(s > 0)
+    def _():
+        to_next.wait_recv()
+
+    carried = edge_in[...].astype(F32)[TAIL - 1 : TAIL]
+    opening = wide[0:1] + (carried - wide[0:1]) * blend_ref[...]
+    xk[0:half] = jnp.where(iota((half, width), 0) == 0, opening, mixed[0:half]).astype(BF16)
+    phase_z(0)
 
     def phase_a(c):
         def start_a(i):
@@ -527,23 +543,23 @@
 
         others(step)
 
-    phase_a(0)
+    phase_a(1)
     keep1.wait()
     keep2.wait()
     for e in range(1, q):
         for c in take_weight(e):
             c.wait_recv()
+    phase_b(1)
+    phase_a(0)
     phase_b(0)
-    phase_a(1)
-    phase_b(1)
+    phase_c(1)
     phase_c(0)
-    phase_c(1)
+    phase_d(1)
     phase_d(0)
-    phase_d(1)
+    phase_y(1)
     phase_y(0)
-    phase_y(1)
-
-    for c in range(2):
+
+    for c in (1, 0):
         loop(1, n_hid, lambda i: take_y(c, ring(h, i, n_hid)).wait_recv())
         span = slice(c * half, (c + 1) * half)
 

time: 132 us -> 127 us (0.962)
  Pallas kernels: 129 us -> 123 us
    pallas_call x1, Pallas kernels: 129 us -> 123 us  [local(): pl.pallas_call(functools.partial(block_kernel, n_seq, n_hid, head), out_s...]
where the time goes in v4:
time: 127 us
  Pallas kernels  123 us (97%)
  local copies, waits for them, and re-layouts  3.03 us (2%)
    pallas_call x1, Pallas kernels, local(): pl.pallas_call(functools.partial(block_kernel, n_seq, n_hid, head), out_s...  123 us

profile of v4, /device:TPU:24, one launch (start us, length us, event | category | flops | bytes accessed | tf_op | source)
XLA Modules:
  0.0 126.5 jit_solution(1494001653455229867)
XLA Ops:
  0.0 1.4 %reshape.18.boost_hbm = f32[1,1024]{1,0:T(1,128)} reshape(f32[16,64]{1,0:T(8,128)} %param.20) | data formatting | bytes 8192 | tf_op jit(solution)/shard_map/reshape | solution.py:611
  1.4 123.5 %shard_map.136 = bf16[128,1024]{1,0:T(8,128)(2,1)} custom-call(bf16[128,1024]{1,0:T(8,128)(2,1)} %skip_hbm.1, bf16[128,1024]{1,0:T(8,128)(2,1)} %r_hbm.1, bf16[128,1024]{1,0:T(8,128)(2,1)} %k_hbm.1, bf16[128,1024]{1,0:T(8,128)(2,1)} %v_hbm.1, bf16[128,1024]{1,0:T(8,128)(2,1)} %gate_hbm.1, f32[128,1024]{1,0:T(8,128)} %logit_hbm.1, ...), custom_call_target="tpu_custom_call" | custom-call | tf_op jit(solution)/shard_map/pallas_call | solution.py:612
  124.9 1.7 %copy.16 = bf16[128,1024]{1,0:T(8,128)(2,1)} copy(bf16[128,1024]{1,0:T(8,128)(2,1)} %shard_map.136) | data formatting | bytes 524288

commit v5 on v4

--- a/solution.py
+++ b/solution.py
@@ -115,7 +115,7 @@
     depth, units = w1_ref.shape
     q = n_seq // n_hid
     pairs = width // LANES
-    half = rows // 2
+    half = rows // 4
     s = lax.axis_index("seq")
     h = lax.axis_index("hid")
     g = lax.div(s, q)
@@ -422,7 +422,8 @@
         loop(1, n_hid, lambda i: send_z(c, i).start())
         planes[c, h] = xk[c * half : (c + 1) * half]
 
-    phase_z(1)
+    for c in range(1, 4):
+        phase_z(c)
 
     @pl.when(s == 0)
     def _():
@@ -550,16 +551,14 @@
         for c in take_weight(e):
             c.wait_recv()
     phase_b(1)
-    phase_a(0)
-    phase_b(0)
-    phase_c(1)
-    phase_c(0)
-    phase_d(1)
-    phase_d(0)
-    phase_y(1)
-    phase_y(0)
-
-    for c in (1, 0):
+    for c in (2, 3, 0):
+        phase_a(c)
+        phase_b(c)
+    for phase in (phase_c, phase_d, phase_y):
+        for c in (1, 2, 3, 0):
+            phase(c)
+
+    for c in (1, 2, 3, 0):
         loop(1, n_hid, lambda i: take_y(c, ring(h, i, n_hid)).wait_recv())
         span = slice(c * half, (c + 1) * half)
 
@@ -588,7 +587,7 @@
 
     def end_sends(i):
         far = ring(g, i, n_hid)
-        for c in range(2):
+        for c in range(4):
             send_z(c, i).wait_send()
             for send in (send_a, send_b, send_c, send_d):
                 send(c, far).wait_send()
@@ -629,16 +628,16 @@
             pltpu.VMEM((TAIL, width), BF16),
             pltpu.VMEM((n_seq, width), F32),
             pltpu.VMEM((rows, width), BF16),
-            pltpu.VMEM((2, n_hid, rows // 2, width), BF16),
-            pltpu.VMEM((2, n_hid, rows // 2, width), BF16),
+            pltpu.VMEM((4, n_hid, rows // 4, width), BF16),
+            pltpu.VMEM((4, n_hid, rows // 4, width), BF16),
             pltpu.VMEM((q, depth, units), BF16),
             pltpu.VMEM((q, depth, units), BF16),
-            pltpu.VMEM((2, n_hid, rows // 2, units), BF16),
-            pltpu.VMEM((2, n_hid, rows // 2, units), BF16),
-            pltpu.VMEM((2, n_hid, rows // 2, units), BF16),
-            pltpu.VMEM((2, n_hid, rows // 2, width), BF16),
-            pltpu.VMEM((2, n_hid, rows // 2, width), BF16),
-            pltpu.VMEM((2, n_hid, rows // 2, width), BF16),
+            pltpu.VMEM((4, n_hid, rows // 4, units), BF16),
+            pltpu.VMEM((4, n_hid, rows // 4, units), BF16),
+            pltpu.VMEM((4, n_hid, rows // 4, units), BF16),
+            pltpu.VMEM((4, n_hid, rows // 4, width), BF16),
+            pltpu.VMEM((4, n_hid, rows // 4, width), BF16),
+            pltpu.VMEM((4, n_hid, rows // 4, width), BF16),
             dma((n_hid,)),
             dma((n_hid,)),
             dma((q * n_hid,)),
@@ -650,18 +649,18 @@
             dma((2, q)),
             dma((2, q)),
             dma((2,)),
-            dma((2, n_hid)),
-            dma((2, n_hid)),
-            dma((2, n_hid)),
-            dma((2, n_hid)),
-            dma((2, n_hid)),
-            dma((2, n_hid)),
-            dma((2, n_hid)),
-            dma((2, n_hid)),
-            dma((2, n_hid)),
-            dma((2, n_hid)),
-            dma((2, n_hid)),
-            dma((2, n_hid)),
+            dma((4, n_hid)),
+            dma((4, n_hid)),
+            dma((4, n_hid)),
+            dma((4, n_hid)),
+            dma((4, n_hid)),
+            dma((4, n_hid)),
+            dma((4, n_hid)),
+            dma((4, n_hid)),
+            dma((4, n_hid)),
+            dma((4, n_hid)),
+            dma((4, n_hid)),
+            dma((4, n_hid)),
         ],
         compiler_params=pltpu.CompilerParams(
             collective_id=0, has_side_effects=True, vmem_limit_bytes=60 * 2**20

time: 127 us -> 117 us (0.921)
  Pallas kernels: 123 us -> 113 us
    pallas_call x1, Pallas kernels: 123 us -> 113 us  [local(): pl.pallas_call(functools.partial(block_kernel, n_seq, n_hid, head), out_s...]
where the time goes in v5:
time: 117 us
  Pallas kernels  113 us (97%)
  local copies, waits for them, and re-layouts  3.03 us (3%)
    pallas_call x1, Pallas kernels, local(): pl.pallas_call(functools.partial(block_kernel, n_seq, n_hid, head), out_s...  113 us

profile of v5, /device:TPU:24, one launch (start us, length us, event | category | flops | bytes accessed | tf_op | source)
XLA Modules:
  0.0 116.5 jit_solution(7308705972763526790)
XLA Ops:
  0.0 1.4 %reshape.18.boost_hbm = f32[1,1024]{1,0:T(1,128)} reshape(f32[16,64]{1,0:T(8,128)} %param.20) | data formatting | bytes 8192 | tf_op jit(solution)/shard_map/reshape | solution.py:610
  1.4 113.5 %shard_map.136 = bf16[128,1024]{1,0:T(8,128)(2,1)} custom-call(bf16[128,1024]{1,0:T(8,128)(2,1)} %skip_hbm.1, bf16[128,1024]{1,0:T(8,128)(2,1)} %r_hbm.1, bf16[128,1024]{1,0:T(8,128)(2,1)} %k_hbm.1, bf16[128,1024]{1,0:T(8,128)(2,1)} %v_hbm.1, bf16[128,1024]{1,0:T(8,128)(2,1)} %gate_hbm.1, f32[128,1024]{1,0:T(8,128)} %logit_hbm.1, ...), custom_call_target="tpu_custom_call" | custom-call | tf_op jit(solution)/shard_map/pallas_call | solution.py:611
  114.8 1.7 %copy.16 = bf16[128,1024]{1,0:T(8,128)(2,1)} copy(bf16[128,1024]{1,0:T(8,128)(2,1)} %shard_map.136) | data formatting | bytes 524288
